TPU v7x, 32 devices: a whole 2x2x4 slice. The times are simulated.
32 devices in a mesh: prompt: 8 (over y, x, core), resp: 4 (over z).
Axes of the slice: x: 2, y: 2, z: 4, core: 2. Of those that a mesh axis runs over, the one named last changes fastest.
Arguments:
- queries: bfloat16 [4096, 2048], P(('prompt', 'resp'))
- resp_keys: bfloat16 [4096, 2048], P(('prompt', 'resp')), may hold values from -6 to 6
- resp_values: bfloat16 [4096, 2048], P(('prompt', 'resp')), may hold values from -6 to 6
- grad_out: bfloat16 [4096, 2048], P(('prompt', 'resp')), may hold values from -3 to 3
- prefix_keys: bfloat16 [2048, 2048], P(('prompt', 'resp'))
- prefix_values: bfloat16 [2048, 2048], P(('prompt', 'resp')), may hold values from -6 to 6
- block_mask: int32 [32, 2], P(('prompt', 'resp')), may hold values from 0 to 1, as said below
- lengths: int32 [32], P(('prompt', 'resp')), may hold values from 1 to 128, as said below
Outputs:
- attended: bfloat16 [4096, 2048], P(('prompt', 'resp'))
- grad_queries: bfloat16 [4096, 2048], P(('prompt', 'resp'))
- grad_resp_keys: bfloat16 [4096, 2048], P(('prompt', 'resp'))
- grad_resp_values: bfloat16 [4096, 2048], P(('prompt', 'resp'))
- grad_prefix_keys: bfloat16 [2048, 2048], P(('prompt', 'resp'))
- grad_prefix_values: bfloat16 [2048, 2048], P(('prompt', 'resp'))
Inputs may be any that keep to these rules, and one draw needn't show every extreme that they name: `block_mask`: column 0 is 1 for every response. `lengths`: the last response of every prompt has length 128.
All inputs are finite; a program needn't handle non-finite values.
Results may differ from a plain program's by a relative error of at most 0.019.
Values may be sent and summed in bfloat16 or wider, within the bound.
A program may use at most 128 MiB of HBM per device.

v0:
```python
import jax
import jax.numpy as jnp
from jax import lax
from jax.sharding import PartitionSpec as P

H = 16
HD = 128
BLK = 128


def key_visibility(mask_row, first_row, count):
    position = (first_row + jnp.arange(count, dtype=jnp.int32)) // BLK
    table = jnp.arange(mask_row.shape[0], dtype=jnp.int32)
    hits = jnp.where(position[:, None] == table[None, :], mask_row[None, :], 0)
    return (jnp.sum(hits, axis=1) > 0)[None, :]


def block_scores(query3, keys3, visible):
    scaling = 1.0 / HD**0.5
    scores = jnp.einsum("shd,khd->hsk", query3, keys3, preferred_element_type=jnp.float32) * scaling
    return jnp.where(visible[None], scores, -jnp.inf)


def statistics_block(carried, query3, keys3, visible):
    running_max, mass_sum = carried
    scores = block_scores(query3, keys3, visible)
    new_max = jnp.maximum(running_max, jnp.max(scores, axis=2))
    mass_sum = mass_sum * jnp.exp(running_max - new_max) + jnp.sum(
        jnp.exp(scores - new_max[..., None]), axis=2
    )
    return (new_max, mass_sum)


def output_block(accumulated, query3, keys3, values3, visible, log_mass):
    scores = block_scores(query3, keys3, visible)
    weights = jnp.exp(scores - log_mass[..., None]).astype(jnp.bfloat16)
    return accumulated + jnp.einsum(
        "hsk,khd->hsd", weights, values3, preferred_element_type=jnp.float32
    )


def backward_block(query3, grads3, keys3, values3, visible, log_mass, delta):
    scaling = 1.0 / HD**0.5
    scores = block_scores(query3, keys3, visible)
    probs = jnp.exp(scores - log_mass[..., None])
    dprob = jnp.einsum("shd,khd->hsk", grads3, values3, preferred_element_type=jnp.float32)
    dscore = (probs * (dprob - delta[..., None])).astype(jnp.bfloat16)
    grad_query = (
        jnp.einsum("hsk,khd->shd", dscore, keys3, preferred_element_type=jnp.float32) * scaling
    )
    grad_key = (
        jnp.einsum("hsk,shd->khd", dscore, query3, preferred_element_type=jnp.float32) * scaling
    )
    grad_value = jnp.einsum(
        "hsk,shd->khd", probs.astype(jnp.bfloat16), grads3, preferred_element_type=jnp.float32
    )
    return (grad_query, grad_key, grad_value)


def on_device(
    queries, resp_keys, resp_values, grad_out, prefix_keys, prefix_values, block_mask, lengths
):
    row_count = queries.shape[0]
    feature_count = queries.shape[1]
    groups = lax.axis_size("resp")
    whole_prefix = prefix_keys.shape[0] * groups
    mask_row = block_mask[0]
    query3 = queries.reshape(row_count, H, HD)
    own_keys3 = resp_keys.reshape(row_count, H, HD)
    own_values3 = resp_values.reshape(row_count, H, HD)
    row_index = jnp.arange(row_count, dtype=jnp.int32)
    gathered_keys, gathered_values = (
        lax.all_gather(prefix_keys, "resp", axis=0, tiled=True),
        lax.all_gather(prefix_values, "resp", axis=0, tiled=True),
    )

    def prefix_blocks():
        blocks = []
        for offset in range(0, whole_prefix, 512):
            span = min(512, whole_prefix - offset)
            blocks.append(
                (
                    gathered_keys[offset : offset + span].reshape(span, H, HD),
                    gathered_values[offset : offset + span].reshape(span, H, HD),
                    key_visibility(mask_row, offset, span),
                )
            )
        return blocks

    def own_blocks():
        span = min(512, row_count)
        visible = row_index[:, None] >= (0 + jnp.arange(span, dtype=jnp.int32))[None, :]
        blocks = [(own_keys3, own_values3, visible)]
        return blocks

    carried = (jnp.full((H, row_count), -1e30, jnp.float32), jnp.zeros((H, row_count), jnp.float32))
    for keys3, values3, visible in prefix_blocks() + own_blocks():
        carried = statistics_block(carried, query3, keys3, visible)
    running_max, mass_sum = carried
    log_mass = running_max + jnp.log(mass_sum)
    accumulated = jnp.zeros((H, row_count, HD), jnp.float32)
    for keys3, values3, visible in prefix_blocks() + own_blocks():
        accumulated = output_block(accumulated, query3, keys3, values3, visible, log_mass)
    attended = (
        jnp.transpose(accumulated, (1, 0, 2)).reshape(row_count, feature_count).astype(jnp.bfloat16)
    )
    valid = row_index < lengths[0]
    grad_scaled = jnp.where(valid[:, None], grad_out, jnp.zeros_like(grad_out))
    grads3 = grad_scaled.reshape(row_count, H, HD)
    delta = jnp.einsum(
        "shd,shd->hs",
        grads3,
        attended.reshape(row_count, H, HD),
        preferred_element_type=jnp.float32,
    )
    grad_query = jnp.zeros((row_count, H, HD), jnp.float32)
    key_terms = []
    value_terms = []
    for keys3, values3, visible in prefix_blocks():
        span = keys3.shape[0]
        part_query, part_key, part_value = backward_block(
            query3, grads3, keys3, values3, visible, log_mass, delta
        )
        grad_query = grad_query + part_query
        key_terms.append(part_key.reshape(span, feature_count))
        value_terms.append(part_value.reshape(span, feature_count))
    grad_keys = jnp.concatenate(key_terms, 0)
    grad_values = jnp.concatenate(value_terms, 0)
    summed_keys, summed_values = (
        lax.psum_scatter(
            grad_keys.astype(jnp.bfloat16), "resp", scatter_dimension=0, tiled=True
        ).astype(jnp.float32),
        lax.psum_scatter(
            grad_values.astype(jnp.bfloat16), "resp", scatter_dimension=0, tiled=True
        ).astype(jnp.float32),
    )
    own_grad_keys = []
    own_grad_values = []
    for keys3, values3, visible in own_blocks():
        span = keys3.shape[0]
        part_query, part_key, part_value = backward_block(
            query3, grads3, keys3, values3, visible, log_mass, delta
        )
        grad_query = grad_query + part_query
        own_grad_keys.append(part_key.reshape(span, feature_count))
        own_grad_values.append(part_value.reshape(span, feature_count))
    grad_resp_keys = own_grad_keys[0].astype(jnp.bfloat16)
    grad_resp_values = own_grad_values[0].astype(jnp.bfloat16)
    grad_queries = grad_query.reshape(row_count, feature_count).astype(jnp.bfloat16)
    return (
        attended,
        grad_queries,
        grad_resp_keys,
        grad_resp_values,
        summed_keys.astype(jnp.bfloat16),
        summed_values.astype(jnp.bfloat16),
    )


def solution(mesh):
    placed = (
        P(("prompt", "resp"), None),
        P(("prompt", "resp"), None),
        P(("prompt", "resp"), None),
        P(("prompt", "resp"), None),
        P(("prompt", "resp"), None),
        P(("prompt", "resp"), None),
        P(("prompt", "resp"), None),
        P(("prompt", "resp")),
    )
    return jax.shard_map(
        on_device,
        mesh=mesh,
        in_specs=placed,
        out_specs=(
            P(("prompt", "resp"), None),
            P(("prompt", "resp"), None),
            P(("prompt", "resp"), None),
            P(("prompt", "resp"), None),
            P(("prompt", "resp"), None),
            P(("prompt", "resp"), None),
        ),
        check_vma=False,
    )
```

profile of v0, /device:TPU:0, one launch (start us, length us, event | category | flops | bytes accessed | tf_op | source)
XLA Modules:
  0.0 141.4 jit_solution(622241191467412037)
XLA Ops:
  7.2 0.0 copy-start
  7.2 0.0 all-gather.3.cloned.1.call-start
  7.2 0.7 all-gather.3.cloned.1.call-update
  7.9 0.0 all-gather.5.cloned.1.call-start
  8.0 0.7 all-gather.5.cloned.1.call-update
  8.7 0.0 reduce-scatter.3.cloned.1.call-start
  9.4 1.1 select_bitcast_fusion
  10.5 0.1 copy.137
  10.7 0.0 copy-start.15
  10.7 0.0 copy-start.16
  10.7 0.1 bitcast_convert_fusion
  10.8 0.1 fusion.18
  10.9 1.4 %copy.129 = f32[16,128,128]{1,2,0:T(8,128)} copy(f32[16,128,128]{2,0,1:T(8,128)S(1)} %bitcast_convert_fusion) | data formatting | bytes 2097152
  12.3 0.3 copy.134
  12.6 0.3 copy.135
  12.9 0.5 copy.111
  13.4 1.4 fusion.21
  14.8 25.5 %all-gather.3.cloned.1.call-done = bf16[256,2048]{1,0:T(8,128)(2,1)} async-done(((bf16[64,2048]{1,0:T(8,128)(2,1)}), bf16[256,2048]{1,0:T(8,128)(2,1)}) %all-gather.3.cloned.1.call-update) | async-done | bytes 1048592 | tf_op jit(solution)/shard_map/all_gather | solution.py:73
  40.3 2.2 %copy.94 = bf16[256,2048]{0,1:T(8,128)(2,1)} copy(bf16[256,2048]{1,0:T(8,128)(2,1)} %all-gather.3.cloned.1.call-done) | data formatting | bytes 2097152 | tf_op jit(solution)/shard_map/all_gather | solution.py:73
  42.5 2.0 %fusion.20 = (f32[16,128]{1,0:T(8,128)S(1)}, f32[16,128,256]{2,1,0:T(8,128)S(1)}) fusion(bf16[128,16,128]{0,2,1:T(8,128)(2,1)} %bitcast.66, bf16[256,16,128]{0,2,1:T(8,128)(2,1)} %bitcast.69, pred[256]{0:T(512)(128)(4,1)S(1)} %broadcast_compare_fusion), kind=kOutput, calls=%fused_computation.43 | convolution fusion | flops 135788544 | bytes 3678464 | tf_op jit(solution)/shard_map/shd,khd->hsk/dot_general | solution.py:20
  44.6 0.2 exponential_reduce_fusion.1
  44.7 0.6 exponential_reduce_fusion
  45.4 23.9 %all-gather.5.cloned.1.call-done = bf16[256,2048]{1,0:T(8,128)(2,1)} async-done(((bf16[64,2048]{1,0:T(8,128)(2,1)}), bf16[256,2048]{1,0:T(8,128)(2,1)}) %all-gather.5.cloned.1.call-update) | async-done | bytes 1048592 | tf_op jit(solution)/shard_map/all_gather | solution.py:74
  69.3 2.3 %copy.99 = bf16[256,2048]{0,1:T(8,128)(2,1)} copy(bf16[256,2048]{1,0:T(8,128)(2,1)} %all-gather.5.cloned.1.call-done) | data formatting | bytes 2097152 | tf_op jit(solution)/shard_map/all_gather | solution.py:74
  71.6 1.9 %fusion.14 = f32[16,128,128]{1,2,0:T(8,128)S(1)} fusion(bf16[256,16,128]{0,2,1:T(8,128)(2,1)} %bitcast.71, f32[16,128,256]{2,1,0:T(8,128)S(1)} %get-tuple-element.33, f32[16,128]{1,0:T(8,128)S(1)} %log_add_fusion), kind=kOutput, calls=%fused_computation.30 | convolution fusion | flops 135266304 | bytes 4202496 | tf_op jit(solution)/shard_map/hsk,khd->hsd/dot_general | solution.py:37
  73.5 1.2 multiply_reduce_fusion
  74.8 1.0 multiply_convert_fusion.1
  75.7 0.1 copy-done.5
  75.8 1.4 multiply_convert_fusion
  77.2 2.3 %copy.114 = bf16[256,2048]{1,0:T(8,128)(2,1)} copy(bf16[256,2048]{0,1:T(8,128)(2,1)} %bitcast.77) | data formatting | bytes 2097152 | tf_op jit(solution)/shard_map/convert_element_type | solution.py:131
  79.4 0.0 reduce-scatter.3.cloned.1.call-update
  79.5 0.0 reduce-scatter.5.cloned.1.call-start
  79.5 1.6 %convolution_convert_fusion = bf16[16,128,256]{2,1,0:T(8,128)(2,1)} fusion(bf16[128,16,128]{0,2,1:T(8,128)(2,1)S(1)} %copy.111, f32[16,128,256]{2,1,0:T(8,128)S(1)} %get-tuple-element.33, f32[16,128]{1,0:T(8,128)S(1)} %log_add_fusion), kind=kOutput, calls=%fused_computation.6 | convolution fusion | flops 135790592 | bytes 3678208 | tf_op jit(solution)/shard_map/hsk,shd->khd/dot_general | solution.py:54
  81.1 2.4 %copy.116 = bf16[256,2048]{1,0:T(8,128)(2,1)} copy(bf16[256,2048]{0,1:T(8,128)(2,1)} %bitcast.76) | data formatting | bytes 2097152 | tf_op jit(solution)/shard_map/convert_element_type | solution.py:134
  83.4 0.0 reduce-scatter.5.cloned.1.call-update
  83.5 2.1 %copy.117 = bf16[128,2048]{1,0:T(8,128)(2,1)} copy(bf16[128,2048]{0,1:T(8,128)(2,1)} %bitcast.81) | data formatting | bytes 1048576
  85.6 0.4 fusion.5
  86.0 0.9 copy-done.9
  86.8 0.4 fusion.22
  87.3 0.8 copy-done.13
  88.1 0.3 fusion.4
  88.4 1.0 copy.118
  89.4 1.5 %fusion.6 = bf16[16,128,128]{1,2,0:T(8,128)(2,1)S(1)} fusion(bf16[16,128,128]{1,2,0:T(8,128)(2,1)} %copy-done.11, bf16[128,16,128]{0,2,1:T(8,128)(2,1)S(1)} %bitcast.68), kind=kOutput, calls=%fused_computation.18 | convolution fusion | flops 67633152 | bytes 1572864 | tf_op jit(solution)/shard_map/hsk,shd->khd/dot_general | solution.py:52
  90.9 1.0 copy.119
  91.9 0.5 convolution_convert_fusion.1
  92.4 1.0 copy.120
  93.4 12.8 %reduce-scatter.3.cloned.1.call-done = bf16[64,2048]{1,0:T(8,128)(2,1)} async-done(((bf16[256,2048]{1,0:T(8,128)(2,1)}), bf16[64,2048]{1,0:T(8,128)(2,1)}) %reduce-scatter.3.cloned.1.call-update) | async-done | bytes 262160 | tf_op jit(solution)/shard_map/reduce_scatter | solution.py:130
  106.3 28.7 %reduce-scatter.5.cloned.1.call-done = bf16[64,2048]{1,0:T(8,128)(2,1)} async-done(((bf16[256,2048]{1,0:T(8,128)(2,1)}), bf16[64,2048]{1,0:T(8,128)(2,1)}) %reduce-scatter.5.cloned.1.call-update) | async-done | bytes 262160 | tf_op jit(solution)/shard_map/reduce_scatter | solution.py:133
  (36 shorter events, 0.1 us)
Async XLA Ops:
  7.2 66.3 %copy-start = (bf16[128,2048]{1,0:T(8,128)(2,1)S(1)}, bf16[128,2048]{1,0:T(8,128)(2,1)}, u32[]{:S(2)}) copy-start(bf16[128,2048]{1,0:T(8,128)(2,1)} %param.10) | copy-start | bytes 1572868
  7.2 3.6 %copy-start.17 = (s32[1,2]{1,0:T(1,128)S(1)}, s32[1,2]{1,0:T(1,128)}, u32[]{:S(2)}) copy-start(s32[1,2]{1,0:T(1,128)} %param.14) | copy-start | bytes 28
  7.2 33.1 %all-gather.3.cloned.1.call-start = ((), (), s32[]{:S(2)}) async-start(), calls=%async_computation.2 | async-start | bytes 1310720 | tf_op jit(solution)/shard_map/all_gather | solution.py:73
  7.9 61.4 %all-gather.5.cloned.1.call-start = ((), (), s32[]{:S(2)}) async-start(), calls=%async_computation.3 | async-start | bytes 1310720 | tf_op jit(solution)/shard_map/all_gather | solution.py:74
  8.7 97.6 %reduce-scatter.3.cloned.1.call-start = ((), (), s32[]{:S(2)}) async-start(), calls=%async_computation.4 | async-start | bytes 1310720 | tf_op jit(solution)/shard_map/reduce_scatter | solution.py:130
  10.7 1.7 %copy-start.15 = (bf16[128,2048]{1,0:T(8,128)(2,1)S(1)}, bf16[128,2048]{1,0:T(8,128)(2,1)}, u32[]{:S(2)}) copy-start(bf16[128,2048]{1,0:T(8,128)(2,1)} %param.8) | copy-start | bytes 1572868
  10.7 1.9 %copy-start.16 = (bf16[128,2048]{1,0:T(8,128)(2,1)S(1)}, bf16[128,2048]{1,0:T(8,128)(2,1)}, u32[]{:S(2)}) copy-start(bf16[128,2048]{1,0:T(8,128)(2,1)} %param.9) | copy-start | bytes 1572868
  12.6 2.2 %copy-start.4 = (bf16[128,2048]{0,1:T(8,128)(2,1)}, bf16[128,2048]{0,1:T(8,128)(2,1)S(1)}, u32[]{:S(2)}) copy-start(bf16[128,2048]{0,1:T(8,128)(2,1)S(1)} %copy.134) | copy-start | bytes 1572868
  12.9 29.6 %copy-start.12 = (bf16[128,2048]{0,1:T(8,128)(2,1)}, bf16[128,2048]{0,1:T(8,128)(2,1)S(1)}, u32[]{:S(2)}) copy-start(bf16[128,2048]{0,1:T(8,128)(2,1)S(1)} %copy.135) | copy-start | bytes 1572868
  42.5 2.1 %copy-start.1 = (f32[16,128,128]{1,2,0:T(8,128)S(1)}, f32[16,128,128]{1,2,0:T(8,128)}, u32[]{:S(2)}) copy-start(f32[16,128,128]{1,2,0:T(8,128)} %get-tuple-element.35) | copy-start | bytes 3145732
  71.5 2.0 %copy-start.2 = (f32[16,128,128]{1,2,0:T(8,128)S(1)}, f32[16,128,128]{1,2,0:T(8,128)}, u32[]{:S(2)}) copy-start(f32[16,128,128]{1,2,0:T(8,128)} %get-tuple-element.35) | copy-start | bytes 3145732
  71.6 2.0 %copy-start.14 = (f32[16,128,128]{1,2,0:T(8,128)S(1)}, f32[16,128,128]{1,2,0:T(8,128)}, u32[]{:S(2)}) copy-start(f32[16,128,128]{1,2,0:T(8,128)} %copy.129) | copy-start | bytes 3145732
  73.5 1.2 copy-start.10
  74.8 1.0 copy-start.5
  75.8 1.4 copy-start.8
  79.5 55.4 %reduce-scatter.5.cloned.1.call-start = ((), (), s32[]{:S(2)}) async-start(), calls=%async_computation.5 | async-start | bytes 1310720 | tf_op jit(solution)/shard_map/reduce_scatter | solution.py:133
  81.1 4.5 %copy-start.3 = (f32[16,128,128]{1,2,0:T(8,128)S(1)}, f32[16,128,128]{1,2,0:T(8,128)}, u32[]{:S(2)}) copy-start(f32[16,128,128]{1,2,0:T(8,128)} %get-tuple-element.35) | copy-start | bytes 3145732
  83.5 2.5 %copy-start.7 = (bf16[256,2048]{0,1:T(8,128)(2,1)S(1)}, bf16[256,2048]{0,1:T(8,128)(2,1)}, u32[]{:S(2)}) copy-start(bf16[256,2048]{0,1:T(8,128)(2,1)} %copy.94) | copy-start | bytes 3145732
  85.6 1.2 copy-start.9
  86.8 1.5 %copy-start.11 = (bf16[16,128,128]{1,2,0:T(8,128)(2,1)}, bf16[16,128,128]{1,2,0:T(8,128)(2,1)S(1)}, u32[]{:S(2)}) copy-start(bf16[16,128,128]{1,2,0:T(8,128)(2,1)S(1)} %fusion.5) | copy-start | bytes 1572868
  86.8 1.2 copy-start.13
  88.1 1.3 copy-start.6
Sparse Core Ops, SparseCore 0:
  9.6 30.6 all-gather.2
  41.8 27.4 all-gather.4
  79.6 26.6 reduce-scatter.2
  109.1 25.7 reduce-scatter.4
where the time goes:
time: 142 us; the launch traced here: 141 us
  waiting for transfers between devices  92.2 us (65%)
  local copies, waits for them, and re-layouts  18.6 us (13%)
  between operations  14.7 us (10%)
  matrix products  13.6 us (10%)
  other arithmetic  2.21 us (2%)
    reduce_scatter x1, waiting for transfers between devices, on_device(): lax.psum_scatter(grad_values.astype(jnp.bfloat16), 'resp', scatter_dimens...  28.7 us
    all_gather x1, waiting for transfers between devices, on_device(): lax.all_gather(prefix_keys, 'resp', axis=0, tiled=True)  25.5 us
    all_gather x1, waiting for transfers between devices, on_device(): lax.all_gather(prefix_values, 'resp', axis=0, tiled=True)  23.9 us
    reduce_scatter x1, waiting for transfers between devices, on_device(): lax.psum_scatter(grad_keys.astype(jnp.bfloat16), 'resp', scatter_dimensio...  12.8 us
    unnamed x42, local copies, waits for them, and re-layouts  8.46 us
    dot_general x2, matrix products, block_scores(): jnp.einsum('shd,khd->hsk', query3, keys3, preferred_element_type=jnp.floa...  3.41 us
    dot_general x2, matrix products, output_block(): jnp.einsum('hsk,khd->hsd', weights, values3, preferred_element_type=jnp.f...  3.15 us
    dot_general x2, matrix products, backward_block(): jnp.einsum('hsk,shd->khd', dscore, query3, preferred_element_type=jnp.flo...  2.91 us
  transfers between devices with their start and end apart: 4, of which 4 were waited for; matrix products, arithmetic and copies ran while one was open for 16% of the time, Pallas kernels for 0%

commit v1 on v0

v1 whole, which is shorter than its diff:
```python
import functools

import jax
import jax.numpy as jnp
from jax import lax
from jax.experimental import pallas as pl
from jax.experimental.pallas import tpu as pltpu
from jax.sharding import PartitionSpec as P

HD = 128
BLK = 128
WIDTH = 256
AHEAD = 2
MESH = pl.DeviceIdType.MESH

GATHER_RIGHT, GATHER_LEFT, SUM_RIGHT, SUM_LEFT = 0, 1, 2, 3


def kernel(
    groups,
    mask_ref,
    length_ref,
    q_hbm,
    k_hbm,
    v_hbm,
    g_hbm,
    pk_hbm,
    pv_hbm,
    att_hbm,
    gq_hbm,
    gk_hbm,
    gv_hbm,
    gpk_hbm,
    gpv_hbm,
    kv,
    ins,
    outs,
    term,
    from_left,
    from_right,
    summed,
    total,
    visible,
    send_sem,
    recv_sem,
    prefix_sem,
    in_sem,
    out_sem,
    sum_sem,
):
    me = lax.axis_index("resp")
    chunks, _, _, span, width = kv.shape
    rows = ins.shape[2]
    prefix = groups * span
    last = groups - 1
    has_left = me > 0
    has_right = me < last

    def columns(c):
        return pl.ds(pl.multiple_of(c * width, width), width)

    def prefix_copy(c, which):
        source = (pk_hbm, pv_hbm)[which]
        return pltpu.make_async_copy(
            source.at[:, columns(c)], kv.at[c, me, which], prefix_sem.at[c, which]
        )

    def in_copy(c, which):
        source = (q_hbm, k_hbm, v_hbm, g_hbm)[which]
        return pltpu.make_async_copy(
            source.at[:, columns(c)], ins.at[which, c], in_sem.at[c, which]
        )

    def out_copy(c, which):
        target = (att_hbm, gq_hbm, gk_hbm, gv_hbm)[which]
        return pltpu.make_async_copy(
            outs.at[which, c], target.at[:, columns(c)], out_sem.at[c, which]
        )

    def sum_copy(c, which):
        target = (gpk_hbm, gpv_hbm)[which]
        return pltpu.make_async_copy(
            summed.at[c, which], target.at[:, columns(c)], sum_sem.at[c, which]
        )

    def remote(kind, c, slot):
        buffer = (kv, kv, from_left, from_right)[kind]
        to = me + 1 if kind in (GATHER_RIGHT, SUM_RIGHT) else me - 1
        return pltpu.make_async_remote_copy(
            src_ref=buffer.at[c, slot],
            dst_ref=buffer.at[c, slot],
            send_sem=send_sem.at[kind, c, slot],
            recv_sem=recv_sem.at[kind, c, slot],
            device_id={"resp": to},
            device_id_type=MESH,
        )

    def send_own(c):
        for which in range(2):
            prefix_copy(c, which).wait()

        @pl.when(has_right)
        def _():
            remote(GATHER_RIGHT, c, me).start()

        @pl.when(has_left)
        def _():
            remote(GATHER_LEFT, c, me).start()

    def start_prefix(c, carry):
        for which in range(2):
            prefix_copy(c, which).start()
        return carry

    def start_ins(c, carry):
        for which in range(4):
            in_copy(c, which).start()
        return carry

    lax.fori_loop(0, chunks, start_prefix, 0)
    barrier = pltpu.get_barrier_semaphore()

    @pl.when(has_left)
    def _():
        pl.semaphore_signal(barrier, inc=1, device_id={"resp": me - 1}, device_id_type=MESH)

    @pl.when(has_right)
    def _():
        pl.semaphore_signal(barrier, inc=1, device_id={"resp": me + 1}, device_id_type=MESH)

    @pl.when(has_left & has_right)
    def _():
        pl.semaphore_wait(barrier, 2)

    @pl.when(jnp.logical_not(has_left & has_right))
    def _():
        pl.semaphore_wait(barrier, 1)

    for c in range(AHEAD):
        send_own(c)
    lax.fori_loop(0, chunks, start_ins, 0)

    key_at = lax.broadcasted_iota(jnp.int32, (rows, prefix + rows), 1)
    row_at = lax.broadcasted_iota(jnp.int32, (rows, prefix + rows), 0)
    seen = jnp.where(key_at - prefix <= row_at, 1, 0)
    for block in range(prefix // BLK):
        inside = (key_at >= block * BLK) & (key_at < (block + 1) * BLK)
        seen = jnp.where(inside, mask_ref[0, block], seen)
    visible[...] = seen
    scaling = 1.0 / HD**0.5

    def gather(c):
        for hop in range(1, groups):

            @pl.when(me - hop >= 0)
            def _():
                remote(GATHER_RIGHT, c, me - hop).wait_recv()

                @pl.when(has_right)
                def _():
                    remote(GATHER_RIGHT, c, me - hop).start()

            @pl.when(me + hop <= last)
            def _():
                remote(GATHER_LEFT, c, me + hop).wait_recv()

                @pl.when(has_left)
                def _():
                    remote(GATHER_LEFT, c, me + hop).start()

    def attend(c):
        for which in range(4):
            in_copy(c, which).wait()
        valid = lax.broadcasted_iota(jnp.int32, (rows, HD), 0) < length_ref[0]
        for head in range(width // HD):
            at = slice(head * HD, (head + 1) * HD)
            query = ins[0, c, :, at]
            keys = jnp.concatenate(
                [kv[c, :, 0, :, at].reshape(prefix, HD), ins[1, c, :, at]], axis=0
            )
            values = jnp.concatenate(
                [kv[c, :, 1, :, at].reshape(prefix, HD), ins[2, c, :, at]], axis=0
            )
            grad32 = jnp.where(valid, ins[3, c, :, at].astype(jnp.float32), 0.0)
            grad = grad32.astype(jnp.bfloat16)
            across = (((1,), (1,)), ((), ()))
            down = (((0,), (0,)), ((), ()))
            scores = (
                lax.dot_general(query, keys, across, preferred_element_type=jnp.float32) * scaling
            )
            scores = jnp.where(visible[...] > 0, scores, -jnp.inf)
            powers = jnp.exp(scores - jnp.max(scores, axis=1, keepdims=True))
            probs = powers * (1.0 / jnp.sum(powers, axis=1, keepdims=True))
            weights = probs.astype(jnp.bfloat16)
            attended = jnp.dot(weights, values, preferred_element_type=jnp.float32).astype(
                jnp.bfloat16
            )
            outs[0, c, :, at] = attended
            delta = jnp.sum(grad32 * attended.astype(jnp.float32), axis=1, keepdims=True)
            dprob = lax.dot_general(grad, values, across, preferred_element_type=jnp.float32)
            dscore = (probs * (dprob - delta)).astype(jnp.bfloat16)
            grad_query = jnp.dot(dscore, keys, preferred_element_type=jnp.float32) * scaling
            outs[1, c, :, at] = grad_query.astype(jnp.bfloat16)
            grad_key = (
                lax.dot_general(dscore, query, down, preferred_element_type=jnp.float32) * scaling
            ).astype(jnp.bfloat16)
            grad_value = lax.dot_general(
                weights, grad, down, preferred_element_type=jnp.float32
            ).astype(jnp.bfloat16)
            term[c, :, 0, :, at] = grad_key[:prefix].reshape(groups, span, HD)
            term[c, :, 1, :, at] = grad_value[:prefix].reshape(groups, span, HD)
            outs[2, c, :, at] = grad_key[prefix:]
            outs[3, c, :, at] = grad_value[prefix:]
        for which in range(4):
            out_copy(c, which).start()

    def relay(kind, buffer, c, slot, receives):
        @pl.when(receives)
        def _():
            remote(kind, c, slot).wait_recv()
            buffer[c, slot] = (
                buffer[c, slot].astype(jnp.float32) + term[c, slot].astype(jnp.float32)
            ).astype(jnp.bfloat16)

        @pl.when(jnp.logical_not(receives))
        def _():
            buffer[c, slot] = term[c, slot]

        remote(kind, c, slot).start()

    def finish(c):
        total[...] = term[c, me].astype(jnp.float32)

        @pl.when(has_left)
        def _():
            remote(SUM_RIGHT, c, me).wait_recv()
            total[...] += from_left[c, me].astype(jnp.float32)

        @pl.when(has_right)
        def _():
            remote(SUM_LEFT, c, me).wait_recv()
            total[...] += from_right[c, me].astype(jnp.float32)

        summed[c] = total[...].astype(jnp.bfloat16)
        for which in range(2):
            sum_copy(c, which).start()
        for hop in range(groups):

            @pl.when((me - hop >= 0) & has_right)
            def _():
                remote(GATHER_RIGHT, c, me - hop).wait_send()

            @pl.when((me + hop <= last) & has_left)
            def _():
                remote(GATHER_LEFT, c, me + hop).wait_send()

            if hop > 0:

                @pl.when(me + hop <= last)
                def _():
                    remote(SUM_RIGHT, c, me + hop).wait_send()

                @pl.when(me - hop >= 0)
                def _():
                    remote(SUM_LEFT, c, me - hop).wait_send()

        for which in range(4):
            out_copy(c, which).wait()

    def step(it, carry):
        @pl.when(it + AHEAD < chunks)
        def _():
            send_own(it + AHEAD)

        @pl.when(it < chunks)
        def _():
            gather(it)
            attend(it)

        right_chunk = it - me
        left_chunk = it - (last - me)

        for hop in range(last, 0, -1):

            @pl.when((me + hop <= last) & (right_chunk >= 0) & (right_chunk < chunks))
            def _():
                relay(SUM_RIGHT, from_left, right_chunk, me + hop, has_left)

            @pl.when((me - hop >= 0) & (left_chunk >= 0) & (left_chunk < chunks))
            def _():
                relay(SUM_LEFT, from_right, left_chunk, me - hop, has_right)

        @pl.when(it >= last)
        def _():
            finish(it - last)

        return carry

    lax.fori_loop(0, chunks + last, step, 0)

    def drain(c, carry):
        for which in range(2):
            sum_copy(c, which).wait()
        return carry

    lax.fori_loop(0, chunks, drain, 0)


def on_device(
    queries, resp_keys, resp_values, grad_out, prefix_keys, prefix_values, block_mask, lengths
):
    rows, features = queries.shape
    span = prefix_keys.shape[0]
    groups = lax.axis_size("resp")
    chunks = features // WIDTH
    anywhere = pl.BlockSpec(memory_space=pl.ANY)
    scalars = pl.BlockSpec(memory_space=pltpu.SMEM)
    shared = (chunks, groups, 2, span, WIDTH)
    per_row = jax.ShapeDtypeStruct(queries.shape, jnp.bfloat16)
    per_prefix = jax.ShapeDtypeStruct(prefix_keys.shape, jnp.bfloat16)
    keys = groups * span + rows
    return pl.pallas_call(
        functools.partial(kernel, groups),
        out_shape=(per_row,) * 4 + (per_prefix,) * 2,
        in_specs=[scalars] * 2 + [anywhere] * 6,
        out_specs=(anywhere,) * 6,
        scratch_shapes=[
            pltpu.VMEM(shared, jnp.bfloat16),
            pltpu.VMEM((4, chunks, rows, WIDTH), jnp.bfloat16),
            pltpu.VMEM((4, chunks, rows, WIDTH), jnp.bfloat16),
            pltpu.VMEM(shared, jnp.bfloat16),
            pltpu.VMEM(shared, jnp.bfloat16),
            pltpu.VMEM(shared, jnp.bfloat16),
            pltpu.VMEM((chunks, 2, span, WIDTH), jnp.bfloat16),
            pltpu.VMEM((2, span, WIDTH), jnp.float32),
            pltpu.VMEM((rows, keys), jnp.int32),
            pltpu.SemaphoreType.DMA((4, chunks, groups)),
            pltpu.SemaphoreType.DMA((4, chunks, groups)),
            pltpu.SemaphoreType.DMA((chunks, 2)),
            pltpu.SemaphoreType.DMA((chunks, 4)),
            pltpu.SemaphoreType.DMA((chunks, 4)),
            pltpu.SemaphoreType.DMA((chunks, 2)),
        ],
        compiler_params=pltpu.CompilerParams(
            collective_id=0, has_side_effects=True, vmem_limit_bytes=56 * 2**20
        ),
        cost_estimate=pl.CostEstimate(
            flops=12 * rows * keys * features,
            bytes_accessed=10 * rows * features * 2,
            transcendentals=rows * keys * features // HD,
        ),
        name="shared_prompt_attention",
    )(
        block_mask,
        lengths,
        queries,
        resp_keys,
        resp_values,
        grad_out,
        prefix_keys,
        prefix_values,
    )


def solution(mesh):
    rows = P(("prompt", "resp"), None)
    return jax.shard_map(
        on_device,
        mesh=mesh,
        in_specs=(rows,) * 7 + (P(("prompt", "resp")),),
        out_specs=(rows,) * 6,
        check_vma=False,
    )
```

time: 142 us -> 94.6 us (0.67)
  waiting for transfers between devices: 92.2 us -> 0 us
  Pallas kernels: 0 us -> 85.6 us
  matrix products: 13.6 us -> 0 us
  between operations: 14.7 us -> 1.3 us
  local copies, waits for them, and re-layouts: 18.6 us -> 7.24 us
  other arithmetic: 2.21 us -> 0 us
    pallas_call x0 -> x1, Pallas kernels: none -> 85.6 us  [on_device(): pl.pallas_call(functools.partial(kernel, groups), out_shape=(per_row,) *...]
    all_gather x2 -> x0, waiting for transfers between devices: 49.3 us -> none  [the longest x1 25.5 us: on_device(): lax.all_gather(prefix_keys, 'resp', axis=0, tiled=True)]
    reduce_scatter x2 -> x0, waiting for transfers between devices: 41.5 us -> none  [the longest x1 28.7 us: on_device(): lax.psum_scatter(grad_values.astype(jnp.bfloat16), 'resp', scatter_dimens...]
    dot_general x12 -> x0, matrix products: 13.6 us -> none  [the longest x2 3.41 us: block_scores(): jnp.einsum('shd,khd->hsk', query3, keys3, preferred_element_type=jnp.floa...]
    convert_element_type x2 -> x0, local copies, waits for them, and re-layouts: 4.61 us -> none  [the longest x1 2.35 us: on_device(): grad_values.astype(jnp.bfloat16)]
    all_gather x2 -> x0, local copies, waits for them, and re-layouts: 4.51 us -> none  [the longest x1 2.26 us: on_device(): lax.all_gather(prefix_values, 'resp', axis=0, tiled=True)]
    unnamed x42 -> x16, local copies, waits for them, and re-layouts: 8.46 us -> 7.24 us
  transfers between devices with their start and end apart: 4 -> 0, of which waited for: 4 -> 0; matrix products, arithmetic and copies ran while one was open for 16% -> 0% of each run, Pallas kernels for 0% -> 0%
where the time goes in v1:
time: 94.6 us; the launch traced here: 94.2 us
  Pallas kernels  85.6 us (90%)
  local copies, waits for them, and re-layouts  7.24 us (8%)
  between operations  1.3 us (1%)
    pallas_call x1, Pallas kernels, on_device(): pl.pallas_call(functools.partial(kernel, groups), out_shape=(per_row,) *...  85.6 us
    unnamed x16, local copies, waits for them, and re-layouts  7.24 us

profile of v1, /device:TPU:0, one launch (start us, length us, event | category | flops | bytes accessed | tf_op | source)
XLA Modules:
  0.0 94.2 jit_solution(17681439065778897392)
XLA Ops:
  1.3 85.6 %shared_prompt_attention.1 = (bf16[128,2048]{1,0:T(8,128)(2,1)}, bf16[128,2048]{1,0:T(8,128)(2,1)}, bf16[128,2048]{1,0:T(8,128)(2,1)}, bf16[128,2048]{1,0:T(8,12...) custom-call(s32[1,2]{1,0:T(1,128)} %mask_ref.1, s32[1]{0:T(128)S(6)} %copy.20.length_ref, ...), custom_call_target="tpu_custom_call" | custom-call | flops 1207959552 | bytes 5242880 | tf_op jit(solution)/shard_map/shared_prompt_attention/pallas_call | solution.py:322
  86.9 0.0 copy-start.2
  86.9 1.9 %copy.21 = bf16[128,2048]{1,0:T(8,128)(2,1)} copy(bf16[128,2048]{1,0:T(8,128)(2,1)} %get-tuple-element.12) | data formatting | bytes 1048576
  88.9 0.0 copy-done.2
  88.9 0.0 copy-start.1
  88.9 0.8 copy.22
  89.7 0.4 copy-done.1
  90.1 0.0 copy-start
  90.1 0.8 copy.23
  90.9 0.4 copy-done
  91.3 0.0 copy-start.4
  91.3 0.8 copy.24
  92.1 0.3 copy-done.4
  92.4 0.0 copy-start.3
  92.4 0.7 copy.25
  93.1 0.3 copy-done.3
  93.5 0.7 copy.26
Async XLA Ops:
  86.9 2.0 %copy-start.2 = (bf16[128,2048]{1,0:T(8,128)(2,1)S(1)}, bf16[128,2048]{1,0:T(8,128)(2,1)}, u32[]{:S(2)}) copy-start(bf16[128,2048]{1,0:T(8,128)(2,1)} %get-tuple-element.13) | copy-start | bytes 1572868
  88.9 1.2 %copy-start.1 = (bf16[128,2048]{1,0:T(8,128)(2,1)S(1)}, bf16[128,2048]{1,0:T(8,128)(2,1)}, u32[]{:S(2)}) copy-start(bf16[128,2048]{1,0:T(8,128)(2,1)} %get-tuple-element.14) | copy-start | bytes 1572868
  90.1 1.2 %copy-start = (bf16[128,2048]{1,0:T(8,128)(2,1)S(1)}, bf16[128,2048]{1,0:T(8,128)(2,1)}, u32[]{:S(2)}) copy-start(bf16[128,2048]{1,0:T(8,128)(2,1)} %get-tuple-element.15) | copy-start | bytes 1572868
  91.3 1.1 %copy-start.4 = (bf16[64,2048]{1,0:T(8,128)(2,1)S(1)}, bf16[64,2048]{1,0:T(8,128)(2,1)}, u32[]{:S(2)}) copy-start(bf16[64,2048]{1,0:T(8,128)(2,1)} %get-tuple-element.16) | copy-start | bytes 786436
  92.4 1.0 %copy-start.3 = (bf16[64,2048]{1,0:T(8,128)(2,1)S(1)}, bf16[64,2048]{1,0:T(8,128)(2,1)}, u32[]{:S(2)}) copy-start(bf16[64,2048]{1,0:T(8,128)(2,1)} %get-tuple-element.17) | copy-start | bytes 786436

commit v2 on v1

--- a/solution.py
+++ b/solution.py
@@ -9,8 +9,9 @@
 
 HD = 128
 BLK = 128
-WIDTH = 256
+WIDTH = 512
 AHEAD = 2
+LAG = 2
 MESH = pl.DeviceIdType.MESH
 
 GATHER_RIGHT, GATHER_LEFT, SUM_RIGHT, SUM_LEFT = 0, 1, 2, 3
@@ -277,8 +278,8 @@
             gather(it)
             attend(it)
 
-        right_chunk = it - me
-        left_chunk = it - (last - me)
+        right_chunk = it - LAG * me
+        left_chunk = it - LAG * (last - me)
 
         for hop in range(last, 0, -1):
 
@@ -290,13 +291,13 @@
             def _():
                 relay(SUM_LEFT, from_right, left_chunk, me - hop, has_right)
 
-        @pl.when(it >= last)
-        def _():
-            finish(it - last)
+        @pl.when(it >= LAG * last)
+        def _():
+            finish(it - LAG * last)
 
         return carry
 
-    lax.fori_loop(0, chunks + last, step, 0)
+    lax.fori_loop(0, chunks + LAG * last, step, 0)
 
     def drain(c, carry):
         for which in range(2):
@@ -304,6 +305,11 @@
         return carry
 
     lax.fori_loop(0, chunks, drain, 0)
+
+
+def hand_over(*refs):
+    for source, target in zip(refs[:6], refs[6:]):
+        target[...] = source[...]
 
 
 def on_device(
@@ -319,7 +325,7 @@
     per_row = jax.ShapeDtypeStruct(queries.shape, jnp.bfloat16)
     per_prefix = jax.ShapeDtypeStruct(prefix_keys.shape, jnp.bfloat16)
     keys = groups * span + rows
-    return pl.pallas_call(
+    results = pl.pallas_call(
         functools.partial(kernel, groups),
         out_shape=(per_row,) * 4 + (per_prefix,) * 2,
         in_specs=[scalars] * 2 + [anywhere] * 6,
@@ -360,6 +366,20 @@
         prefix_keys,
         prefix_values,
     )
+    pieces = 4
+    blocks = [
+        pl.BlockSpec((result.shape[0] // pieces, features), lambda at: (at, 0))
+        for result in results
+    ]
+    return pl.pallas_call(
+        hand_over,
+        grid=(pieces,),
+        out_shape=(per_row,) * 4 + (per_prefix,) * 2,
+        in_specs=blocks,
+        out_specs=tuple(blocks),
+        compiler_params=pltpu.CompilerParams(vmem_limit_bytes=56 * 2**20),
+        name="hand_over",
+    )(*results)
 
 
 def solution(mesh):

time: 94.6 us -> 73.9 us (0.78)
  Pallas kernels: 85.6 us -> 72.4 us
  local copies, waits for them, and re-layouts: 7.24 us -> 0 us
    pallas_call x1, Pallas kernels: 85.6 us -> 68.5 us  [on_device(): pl.pallas_call(functools.partial(kernel, groups), out_shape=(per_row,) *...]
    unnamed x16 -> x0, local copies, waits for them, and re-layouts: 7.24 us -> none
    pallas_call x0 -> x1, Pallas kernels: none -> 3.94 us  [on_device(): pl.pallas_call(hand_over, grid=(pieces,), out_shape=(per_row,) * 4 + (per...]
where the time goes in v2:
time: 73.9 us; the launch traced here: 73.7 us
  Pallas kernels  72.4 us (98%)
  between operations  1.29 us (2%)
    pallas_call x1, Pallas kernels, on_device(): pl.pallas_call(functools.partial(kernel, groups), out_shape=(per_row,) *...  68.5 us
    pallas_call x1, Pallas kernels, on_device(): pl.pallas_call(hand_over, grid=(pieces,), out_shape=(per_row,) * 4 + (per...  3.94 us

profile of v2, /device:TPU:0, one launch (start us, length us, event | category | flops | bytes accessed | tf_op | source)
XLA Modules:
  0.0 73.7 jit_solution(11256864022814529121)
XLA Ops:
  1.3 68.5 %shared_prompt_attention.1 = (bf16[128,2048]{1,0:T(8,128)(2,1)}, bf16[128,2048]{1,0:T(8,128)(2,1)}, bf16[128,2048]{1,0:T(8,128)(2,1)}, bf16[128,2048]{1,0:T(8,12...) custom-call(s32[1,2]{1,0:T(1,128)} %mask_ref.1, s32[1]{0:T(128)S(6)} %copy.14.length_ref, ...), custom_call_target="tpu_custom_call" | custom-call | flops 1207959552 | bytes 5242880 | tf_op jit(solution)/shard_map/shared_prompt_attention/pallas_call | solution.py:328
  69.8 3.9 %hand_over.1 = (bf16[128,2048]{1,0:T(8,128)(2,1)}, bf16[128,2048]{1,0:T(8,128)(2,1)}, bf16[128,2048]{1,0:T(8,128)(2,1)}, bf16[128,2048]{1,0:T(8,128)(2,1)}, bf16...) custom-call(bf16[128,2048]{1,0:T(8,128)(2,1)} %get-tuple-element.12.refs_0_, bf16[128,2048]{1,0:T(8,128)(2,1)} %get-tuple-element.13.refs_1_, ...), custom_call_target="tpu_custom_call" | custom-call | tf_op jit(solution)/shard_map/hand_over/pallas_call | solution.py:374

commit v3 on v2

--- a/solution.py
+++ b/solution.py
@@ -11,7 +11,6 @@
 BLK = 128
 WIDTH = 512
 AHEAD = 2
-LAG = 2
 MESH = pl.DeviceIdType.MESH
 
 GATHER_RIGHT, GATHER_LEFT, SUM_RIGHT, SUM_LEFT = 0, 1, 2, 3
@@ -278,8 +277,8 @@
             gather(it)
             attend(it)
 
-        right_chunk = it - LAG * me
-        left_chunk = it - LAG * (last - me)
+        right_chunk = it - me - jnp.where(me > 0, 1, 0)
+        left_chunk = it - (last - me) - jnp.where(me < last, 1, 0)
 
         for hop in range(last, 0, -1):
 
@@ -291,13 +290,13 @@
             def _():
                 relay(SUM_LEFT, from_right, left_chunk, me - hop, has_right)
 
-        @pl.when(it >= LAG * last)
-        def _():
-            finish(it - LAG * last)
+        @pl.when(it >= (last + 1))
+        def _():
+            finish(it - (last + 1))
 
         return carry
 
-    lax.fori_loop(0, chunks + LAG * last, step, 0)
+    lax.fori_loop(0, chunks + (last + 1), step, 0)
 
     def drain(c, carry):
         for which in range(2):

time: 73.9 us -> 73.3 us (level)
  no operation moved by 1% of the time
where the time goes in v3:
time: 73.3 us; the launch traced here: 73.1 us
  Pallas kernels  71.8 us (98%)
  between operations  1.29 us (2%)
    pallas_call x1, Pallas kernels, on_device(): pl.pallas_call(functools.partial(kernel, groups), out_shape=(per_row,) *...  67.9 us
    pallas_call x1, Pallas kernels, on_device(): pl.pallas_call(hand_over, grid=(pieces,), out_shape=(per_row,) * 4 + (per...  3.94 us

profile of v3, /device:TPU:0, one launch (start us, length us, event | category | flops | bytes accessed | tf_op | source)
XLA Modules:
  0.0 73.1 jit_solution(7546481561501999133)
XLA Ops:
  1.3 67.9 %shared_prompt_attention.1 = (bf16[128,2048]{1,0:T(8,128)(2,1)}, bf16[128,2048]{1,0:T(8,128)(2,1)}, bf16[128,2048]{1,0:T(8,128)(2,1)}, bf16[128,2048]{1,0:T(8,12...) custom-call(s32[1,2]{1,0:T(1,128)} %mask_ref.1, s32[1]{0:T(128)S(6)} %copy.14.length_ref, ...), custom_call_target="tpu_custom_call" | custom-call | flops 1207959552 | bytes 5242880 | tf_op jit(solution)/shard_map/shared_prompt_attention/pallas_call | solution.py:327
  69.2 3.9 %hand_over.1 = (bf16[128,2048]{1,0:T(8,128)(2,1)}, bf16[128,2048]{1,0:T(8,128)(2,1)}, bf16[128,2048]{1,0:T(8,128)(2,1)}, bf16[128,2048]{1,0:T(8,128)(2,1)}, bf16...) custom-call(bf16[128,2048]{1,0:T(8,128)(2,1)} %get-tuple-element.12.refs_0_, bf16[128,2048]{1,0:T(8,128)(2,1)} %get-tuple-element.13.refs_1_, ...), custom_call_target="tpu_custom_call" | custom-call | tf_op jit(solution)/shard_map/hand_over/pallas_call | solution.py:373
